TPU v7x, 128 devices: a whole 4x4x4 slice. The times are simulated.
128 devices in a mesh: row: 4 (over y_hi, core), col: 32 (over z, y_lo, x).
Axes of the slice: x: 4, y: 4 (y_hi: 2, y_lo: 2; y = y_hi * 2 + y_lo), z: 4, core: 2. Of those that a mesh axis runs over, the one named last changes fastest.
Arguments:
- slopes: float32 [1024, 131072], P('col', 'row'), may hold values from -6 to 6
- covariance: float32 [2048, 131072], P('row', 'col'), may hold values from -6 to 6
Outputs:
- updated: float32 [2048, 131072], P('row', 'col')
All inputs are finite; a program needn't handle non-finite values.
Results may differ from a plain program's by a relative error of at most 0.00007.
Values sent between devices are 32-bit elements; how exact they have to be, the bound alone decides.
A program may use at most 192 MiB of HBM per device.

v0:
```python
import jax
import jax.numpy as jnp
from jax import lax
from jax.sharding import PartitionSpec as P


def per_device(slopes, covariance):
    slab_rows = covariance.shape[0]
    gathered = lax.all_gather(slopes, "row", axis=1, tiled=True)
    first = lax.axis_index("row") * slab_rows
    slab_local = lax.dynamic_slice_in_dim(gathered, first, slab_rows, 1)
    columns = lax.all_to_all(gathered, "col", split_axis=1, concat_axis=0, tiled=True)
    slab_all = lax.all_gather(slab_local, "col", axis=0, tiled=True)
    product = lax.dot_general(
        slab_all,
        columns,
        (((0,), (0,)), ((), ())),
        precision=lax.Precision.HIGHEST,
        preferred_element_type=jnp.float32,
    )
    total_frames = columns.shape[0]
    return covariance + product / jnp.sqrt(jnp.float32(total_frames))


def solution(mesh):
    in_specs = (P("col", "row"), P("row", "col"))
    out_specs = P("row", "col")
    return jax.shard_map(
        per_device, mesh=mesh, in_specs=in_specs, out_specs=out_specs, check_vma=False
    )
```

profile of v0, /device:TPU:1, one launch (start us, length us, event | category | flops | bytes accessed | tf_op | source)
XLA Modules:
  0.0 468.1 jit_solution(11154313097494166750)
XLA Ops:
  6.5 0.0 all-gather.3.cloned.1.call-start
  6.5 0.7 all-gather.3.cloned.1.call-update
  7.3 115.4 %all-gather.3.cloned.1.call-done = f32[32,131072]{1,0:T(8,128)} async-done(((f32[32,32768]{1,0:T(8,128)}), f32[32,131072]{1,0:T(8,128)}) %all-gather.3.cloned.1.call-update) | async-done | bytes 16777232 | tf_op jit(solution)/shard_map/all_gather | solution.py:9
  122.7 11.6 %copy.7 = f32[4,32,8,4096]{3,2,0,1:T(8,128)} copy(f32[4,32,8,4096]{3,2,1,0:T(8,128)} %bitcast.10) | data formatting | bytes 33554432 | tf_op jit(solution)/shard_map/all_to_all | solution.py:12
  134.3 7.1 %all-to-all-start = ((f32[32,32,4096]{2,0,1:T(8,128)}), f32[32,32,4096]{2,0,1:T(8,128)}, u32[]{:S(2)}, u32[]{:S(2)}) async-start(f32[32,32,4096]{2,0,1:T(8,128)} %bitcast.9), calls=%async_computation | async-start | bytes 33554432 | tf_op jit(solution)/shard_map/all_to_all | solution.py:12
  141.4 0.0 all-gather.5.cloned.1.call-start
  141.4 1.5 constant_dynamic-slice_fusion
  142.9 0.0 all-gather.5.cloned.1.call-update
  142.9 286.4 %all-gather.5.cloned.1.call-done = f32[1024,512]{1,0:T(8,128)} async-done(((f32[32,512]{1,0:T(8,128)}), f32[1024,512]{1,0:T(8,128)}) %all-gather.5.cloned.1.call-update) | async-done | bytes 2097168 | tf_op jit(solution)/shard_map/all_gather | solution.py:13
  429.3 0.0 all-to-all-done
  429.4 32.0 %multiply_add_fusion = f32[512,4096]{1,0:T(8,128)} fusion(f32[512,4096]{1,0:T(8,128)} %param.3, f32[1024,512]{1,0:T(8,128)} %all-gather.5.cloned.1.call-done, f32[1024,4096]{1,0:T(8,128)} %bitcast.1), kind=kOutput, calls=%fused_computation.1 | convolution fusion | flops 25773998080 | bytes 35651584 | tf_op jit(solution)/shard_map/dot_general | solution.py:14
Async XLA Ops:
  6.5 116.1 %all-gather.3.cloned.1.call-start = ((), (), s32[]{:S(2)}) async-start(), calls=%async_computation.1 | async-start | bytes 20971520 | tf_op jit(solution)/shard_map/all_gather | solution.py:9
  134.3 295.1 %all-to-all-start = ((f32[32,32,4096]{2,0,1:T(8,128)}), f32[32,32,4096]{2,0,1:T(8,128)}, u32[]{:S(2)}, u32[]{:S(2)}) async-start(f32[32,32,4096]{2,0,1:T(8,128)} %bitcast.9), calls=%async_computation | async-start | bytes 33554432 | tf_op jit(solution)/shard_map/all_to_all | solution.py:12
  141.4 288.0 %all-gather.5.cloned.1.call-start = ((), (), s32[]{:S(2)}) async-start(), calls=%async_computation.2 | async-start | bytes 2162688 | tf_op jit(solution)/shard_map/all_gather | solution.py:13
Sparse Core Ops, SparseCore 0:
  9.0 113.6 all-gather.2
  143.9 285.4 all-gather.4
where the time goes:
time: 474 us; the launch traced here: 468 us
  waiting for transfers between devices  403 us (85%)
  matrix products  32 us (7%)
  between operations  13.4 us (3%)
  local copies, waits for them, and re-layouts  13.1 us (3%)
  starting transfers between devices  7.15 us (2%)
    all_gather x1, waiting for transfers between devices, per_device(): slab_all = lax.all_gather(slab_local, 'col', axis=0, tiled=True)  286 us
    all_gather x1, waiting for transfers between devices, per_device(): gathered = lax.all_gather(slopes, 'row', axis=1, tiled=True)  115 us
    dot_general x1, matrix products, per_device(): lax.dot_general(slab_all, columns, (((0,), (0,)), ((), ())), precision=la...  32 us
    all_to_all x1, local copies, waits for them, and re-layouts, per_device(): lax.all_to_all(gathered, 'col', split_axis=1, concat_axis=0, tiled=True)  11.6 us
  transfers between devices with their start and end apart: 3, of which 2 were waited for; matrix products, arithmetic and copies ran while one was open for 0% of the time, Pallas kernels for 0%

commit v1 on v0

v1 whole, which is shorter than its diff:
```python
import functools

import jax
import jax.numpy as jnp
from jax import lax
from jax.experimental import pallas as pl
from jax.experimental.pallas import tpu as pltpu
from jax.sharding import PartitionSpec as P

MESH = pl.DeviceIdType.MESH
WIDTH = 256
AHEAD = 3
LAG = 3


def kernel(
    slopes, cov, out, held, tall, slab, slab_hi, slab_lo,
    sx, rx, sy, ry, sf, rf, ss, rs, own_sem, cov_sem,
):
    row, col = lax.axis_index("row"), lax.axis_index("col")
    x, y_lo, z = lax.rem(col, 4), lax.rem(lax.div(col, 4), 2), lax.div(col, 8)
    core, y_hi = lax.rem(row, 2), lax.div(row, 2)
    tiles, frames, width = tall.shape
    half = frames // 2
    block = tiles * width
    depth = slab.shape[3]

    def at(dx, dz):
        return lax.rem(z + dz, 4) * 8 + y_lo * 4 + lax.rem(x + dx, 4)

    barrier = pltpu.get_barrier_semaphore()
    for dr in range(4):
        for dc in range(8):
            if dr or dc:
                there = lax.rem(dc + y_lo + 2 * z, 8)
                pl.semaphore_signal(
                    barrier, inc=1,
                    device_id=(lax.rem(row + dr, 4), there * 4 + x),
                    device_id_type=MESH,
                )
    for dx in range(1, 4):
        pl.semaphore_signal(barrier, inc=1, device_id=(row, at(dx, 0)), device_id_type=MESH)
    pl.semaphore_wait(barrier, 34)

    def remote(src, dst, send, recv, r, c):
        return pltpu.make_async_remote_copy(
            src_ref=src, dst_ref=dst, send_sem=send, recv_sem=recv,
            device_id=(r, c), device_id_type=MESH,
        )

    cov_copy = pltpu.make_async_copy(cov, out, cov_sem)

    is_source = row < 2
    is_source = jnp.logical_and(is_source, core == 0)

    def slab_columns(r):
        return slopes.at[:, pl.ds(pl.multiple_of(r * 512, 512), 512)]

    @pl.when(is_source)
    def _():
        mine = slab.at[y_lo, z, x]
        for dr in range(4):
            for dl in range(2):
                r, l = lax.rem(row + dr, 4), lax.rem(y_lo + dl, 2)
                if dr == 0 and dl == 0:
                    pltpu.make_async_copy(slab_columns(r), mine, rs.at[0]).start()
                else:
                    remote(slab_columns(r), mine, ss.at[0], rs.at[0], r, z * 8 + l * 4 + x).start()

    def slab_z():
        return [
            remote(slab.at[:, z, x], slab.at[:, z, x], ss.at[1], rs.at[1], row, at(0, dz))
            for dz in range(1, 4)
        ]

    def slab_x():
        return [
            remote(slab.at[:, :, x], slab.at[:, :, x], ss.at[2], rs.at[2], row, at(dx, 0))
            for dx in range(1, 4)
        ]

    def wait_for(ref, sem):
        pltpu.make_async_copy(ref, ref, sem).wait()

    def send_x(t):
        for l in range(2):
            for dx in range(4):
                to = lax.rem(x + dx, 4)
                first = pl.multiple_of((l * 4 + to) * block + t * width, width)
                src = slopes.at[:, pl.ds(first, width)]
                dst = held.at[t, l, pl.ds(pl.multiple_of(x * depth, depth), depth)]
                if dx == 0:
                    pltpu.make_async_copy(src, dst, rx.at[t]).start()
                else:
                    remote(src, dst, sx.at[t], rx.at[t], row, at(dx, 0)).start()

    def yz(t, dh, l, start):
        h = lax.rem(y_hi + dh, 2)
        src = held.at[t, l]
        dst = tall.at[t, pl.ds(pl.multiple_of(y_lo * half + z * 128, 128), 128)]
        r, c = h * 2 + y_lo, row * 8 + l * 4 + x
        is_self = jnp.logical_and(r == row, c == col)

        if start:

            @pl.when(is_self)
            def _():
                pltpu.make_async_copy(src, dst, ry.at[t]).start()

        @pl.when(jnp.logical_not(is_self))
        def _():
            copy = remote(src, dst, sy.at[t], ry.at[t], r, c)
            if start:
                copy.start()
            else:
                copy.wait_send()

    def send_yz(t):
        for dh in (1, 0):
            for l in range(2):
                yz(t, dh, l, True)

    def group(t, g):
        return tall.at[t, pl.ds(pl.multiple_of(g * half, half), half)]

    def forward(t):
        mine = group(t, core)
        return remote(mine, mine, sf.at[t], rf.at[t], y_hi * 2 + 1 - core, col)

    def compute(t):
        tile = tall[t]
        hi = tile.astype(jnp.bfloat16)
        lo = (tile - hi.astype(jnp.float32)).astype(jnp.bfloat16)
        dot = functools.partial(jnp.dot, preferred_element_type=jnp.float32)
        product = dot(slab_hi[...], hi) + dot(slab_hi[...], lo) + dot(slab_lo[...], hi)
        columns = pl.ds(pl.multiple_of(t * width, width), width)
        out[:, columns] = out[:, columns] + product * (1.0 / frames**0.5)

    for t in range(AHEAD):
        send_x(t)
    cov_copy.start()
    wait_for(slab.at[:, z, x], rs.at[0])
    for copy in slab_z():
        copy.start()

    def prepare():
        cov_copy.wait()
        wait_for(slab.at[:, :, pl.ds(0, 3)], rs.at[2])
        for l in range(2):
            whole = slab[l].reshape(half, 512).T
            hi = whole.astype(jnp.bfloat16)
            columns = pl.ds(l * half, half)
            slab_hi[:, columns] = hi
            slab_lo[:, columns] = (whole - hi.astype(jnp.float32)).astype(jnp.bfloat16)

    @pl.loop(0, tiles + LAG + 1)
    def _(s):
        @pl.when(s < tiles)
        def _():
            wait_for(held.at[s], rx.at[s])
            send_yz(s)

        @pl.when(s + AHEAD < tiles)
        def _():
            send_x(s + AHEAD)

        @pl.when(s == 0)
        def _():
            wait_for(slab.at[:, pl.ds(0, 3), x], rs.at[1])
            for copy in slab_x():
                copy.start()

        @pl.when(jnp.logical_and(s >= LAG, s < tiles + LAG))
        def _():
            u = s - LAG
            wait_for(group(u, core), ry.at[u])
            forward(u).start()

        @pl.when(s == LAG)
        def _():
            prepare()

        @pl.when(s > LAG)
        def _():
            v = s - LAG - 1
            wait_for(group(v, 1 - core), rf.at[v])
            compute(v)

    @pl.when(is_source)
    def _():
        wait_for(tall.at[0, pl.ds(0, 7 * 64)], ss.at[0])
    for copy in slab_z():
        copy.wait_send()
    for copy in slab_x():
        copy.wait_send()

    @pl.loop(0, tiles)
    def _(t):
        wait_for(held.at[t].at[:, 0:96], sx.at[t])
        for dh in (1, 0):
            for l in range(2):
                yz(t, dh, l, False)
        forward(t).wait_send()


def per_device(slopes, covariance):
    frames, columns, rows = 1024, covariance.shape[1], covariance.shape[0]
    tiles = columns // WIDTH
    vmem = pl.BlockSpec(memory_space=pltpu.VMEM)
    hbm = pl.BlockSpec(memory_space=pl.ANY)
    dma = pltpu.SemaphoreType.DMA
    return pl.pallas_call(
        kernel,
        out_shape=jax.ShapeDtypeStruct(covariance.shape, jnp.float32),
        in_specs=[hbm, hbm],
        out_specs=vmem,
        scratch_shapes=[
            pltpu.VMEM((tiles, 2, 128, WIDTH), jnp.float32),
            pltpu.VMEM((tiles, frames, WIDTH), jnp.float32),
            pltpu.VMEM((2, 4, 4, 32, rows), jnp.float32),
            pltpu.VMEM((rows, frames), jnp.bfloat16),
            pltpu.VMEM((rows, frames), jnp.bfloat16),
            dma((tiles,)), dma((tiles,)), dma((tiles,)), dma((tiles,)), dma((tiles,)), dma((tiles,)),
            dma((3,)), dma((3,)), dma, dma,
        ],
        compiler_params=pltpu.CompilerParams(
            collective_id=0, has_side_effects=True, vmem_limit_bytes=50 << 20
        ),
        cost_estimate=pl.CostEstimate(
            flops=6 * rows * frames * columns, bytes_accessed=24 << 20, transcendentals=0
        ),
        name="slab_update",
    )(slopes, covariance)


def solution(mesh):
    return jax.shard_map(
        per_device, mesh=mesh, in_specs=(P("col", "row"), P("row", "col")),
        out_specs=P("row", "col"), check_vma=False,
    )
```

time: 474 us -> 143 us (0.30); the launches traced: 468 us -> 142 us
  waiting for transfers between devices: 403 us -> 0 us
  Pallas kernels: 0 us -> 135 us
  matrix products: 32 us -> 0 us
  between operations: 13.4 us -> 0.01 us
  starting transfers between devices: 7.15 us -> 0 us
  local copies, waits for them, and re-layouts: 13.1 us -> 7.77 us
    all_gather x2 -> x0, waiting for transfers between devices: 402 us -> none  [the longest x1 286 us: per_device(): slab_all = lax.all_gather(slab_local, 'col', axis=0, tiled=True)]
    pallas_call x0 -> x1, Pallas kernels: none -> 135 us  [per_device(): pl.pallas_call(kernel, out_shape=jax.ShapeDtypeStruct(covariance.shape, j...]
    dot_general x1 -> x0, matrix products: 32 us -> none  [per_device(): lax.dot_general(slab_all, columns, (((0,), (0,)), ((), ())), precision=la...]
    all_to_all x1 -> x0, local copies, waits for them, and re-layouts: 11.6 us -> none  [per_device(): lax.all_to_all(gathered, 'col', split_axis=1, concat_axis=0, tiled=True)]
    unnamed x0 -> x1, local copies, waits for them, and re-layouts: none -> 7.77 us
    all_to_all x1 -> x0, starting transfers between devices: 7.1 us -> none  [per_device(): lax.all_to_all(gathered, 'col', split_axis=1, concat_axis=0, tiled=True)]
  transfers between devices with their start and end apart: 3 -> 0, of which waited for: 2 -> 0; matrix products, arithmetic and copies ran while one was open for 0% -> 0% of each run, Pallas kernels for 0% -> 0%
where the time goes in v1:
time: 143 us; the launch traced here: 142 us
  Pallas kernels  135 us (94%)
  local copies, waits for them, and re-layouts  7.77 us (5%)
    pallas_call x1, Pallas kernels, per_device(): pl.pallas_call(kernel, out_shape=jax.ShapeDtypeStruct(covariance.shape, j...  135 us
    unnamed x1, local copies, waits for them, and re-layouts  7.77 us

profile of v1, /device:TPU:1, one launch (start us, length us, event | category | flops | bytes accessed | tf_op | source)
XLA Modules:
  0.0 142.4 jit_solution(16366825709090005532)
XLA Ops:
  0.0 134.6 %slab_update.1 = f32[512,4096]{1,0:T(8,128)} custom-call(f32[32,32768]{1,0:T(8,128)} %slopes.1, f32[512,4096]{1,0:T(8,128)} %cov.1), custom_call_target="tpu_custom_call" | custom-call | flops 12884901888 | bytes 25165824 | tf_op jit(solution)/shard_map/slab_update/pallas_call | solution.py:212
  134.6 7.8 %copy.4 = f32[512,4096]{1,0:T(8,128)} copy(f32[512,4096]{1,0:T(8,128)} %slab_update.1) | data formatting | bytes 16777216

commit v2 on v1

--- a/solution.py
+++ b/solution.py
@@ -9,8 +9,8 @@
 
 MESH = pl.DeviceIdType.MESH
 WIDTH = 256
-AHEAD = 3
-LAG = 3
+AHEAD = 6
+LAG = 6
 
 
 def kernel(
@@ -211,7 +211,7 @@
     dma = pltpu.SemaphoreType.DMA
     return pl.pallas_call(
         kernel,
-        out_shape=jax.ShapeDtypeStruct(covariance.shape, jnp.float32),
+        out_shape=pltpu.VMEM(covariance.shape, jnp.float32),
         in_specs=[hbm, hbm],
         out_specs=vmem,
         scratch_shapes=[

time: 143 us -> 121 us (0.85)
  Pallas kernels: 135 us -> 117 us
  local copies, waits for them, and re-layouts: 7.77 us -> 3.4 us
    pallas_call x1, Pallas kernels: 135 us -> 117 us  [per_device(): pl.pallas_call(kernel, out_shape=pltpu.VMEM(covariance.shape, jnp.float32...]
    unnamed x1, local copies, waits for them, and re-layouts: 7.77 us -> 3.4 us
where the time goes in v2:
time: 121 us
  Pallas kernels  117 us (97%)
  local copies, waits for them, and re-layouts  3.4 us (3%)
    pallas_call x1, Pallas kernels, per_device(): pl.pallas_call(kernel, out_shape=pltpu.VMEM(covariance.shape, jnp.float32...  117 us
    unnamed x1, local copies, waits for them, and re-layouts  3.4 us

profile of v2, /device:TPU:1, one launch (start us, length us, event | category | flops | bytes accessed | tf_op | source)
XLA Modules:
  0.0 120.7 jit_solution(8534478139470273200)
XLA Ops:
  0.0 117.3 %slab_update.1 = f32[512,4096]{1,0:T(8,128)S(1)} custom-call(f32[32,32768]{1,0:T(8,128)} %slopes.1, f32[512,4096]{1,0:T(8,128)} %cov.1), custom_call_target="tpu_custom_call" | custom-call | flops 12884901888 | bytes 25165824 | tf_op jit(solution)/shard_map/slab_update/pallas_call | solution.py:212
  117.3 3.4 %copy.4 = f32[512,4096]{1,0:T(8,128)} copy(f32[512,4096]{1,0:T(8,128)S(1)} %slab_update.1) | data formatting | bytes 16777216

commit v3 on v0

v3 whole, which is shorter than its diff:
```python
import functools

import jax
import jax.numpy as jnp
from jax import lax
from jax.experimental import pallas as pl
from jax.experimental.pallas import tpu as pltpu
from jax.sharding import PartitionSpec as P

MESH = pl.DeviceIdType.MESH
WIDTH = 512
AHEAD = 2
LAG_Z = 2
LAG = 5
SLAB_X, EVERY = 5, 1
FIRST = 21
ORDER = (2, 1, 3)


def kernel(
    slopes_hbm, cov, out, slopes, held, mid, tall, slab, slab_hi, slab_lo,
    sx, rx, sy, ry, sz, rz, sf, rf, ss, rs, cov_sem, own_sem,
):
    row, col = lax.axis_index("row"), lax.axis_index("col")
    x, y_lo, z = lax.rem(col, 4), lax.rem(lax.div(col, 4), 2), lax.div(col, 8)
    core, y_hi = lax.rem(row, 2), lax.div(row, 2)
    z_odd, z_hi = lax.rem(z, 2), lax.div(z, 2)
    y = y_hi * 2 + y_lo
    units, sources, depth, width = tall.shape
    deep = sources * depth
    block = units // 4 * width
    frames = 4 * deep

    def along_x(dx):
        return row, z * 8 + y_lo * 4 + lax.rem(x + dx, 4)

    def along_y(dy, k):
        to = lax.rem(y + dy, 4)
        return lax.div(to, 2) * 2 + k, z * 8 + lax.rem(to, 2) * 4 + x

    def along_z(dz, k):
        return y_hi * 2 + k, lax.rem(z + dz, 4) * 8 + y_lo * 4 + x

    own_copy = pltpu.make_async_copy(slopes_hbm, slopes, own_sem)
    own_copy.start()

    other = 1 - core
    partners = [along_x(d) for d in (1, 2, 3)] + [along_y(0, other)]
    for d in (1, 2, 3):
        for k in (core, other):
            partners += [along_y(d, k), along_z(d, k)]
    barrier = pltpu.get_barrier_semaphore()
    for partner in partners:
        pl.semaphore_signal(barrier, inc=1, device_id=partner, device_id_type=MESH)
    pl.semaphore_wait(barrier, len(partners))
    own_copy.wait()

    def remote(src, dst, send, recv, to):
        return pltpu.make_async_remote_copy(
            src_ref=src, dst_ref=dst, send_sem=send, recv_sem=recv,
            device_id=to, device_id_type=MESH,
        )

    def wait_for(ref, sem):
        pltpu.make_async_copy(ref, ref, sem).wait()

    cov_copy = pltpu.make_async_copy(cov, out, cov_sem)

    is_source = jnp.logical_and(y_hi == 0, core == 0)

    def slab_columns(r):
        return slopes.at[:, pl.ds(pl.multiple_of(r * 512, 512), 512)]

    @pl.when(is_source)
    def _():
        mine = slab.at[x, z_odd, z_hi, y_lo]
        pltpu.make_async_copy(slab_columns(row), mine, rs.at[0]).start()
        for dy, k in ((0, 1), (1, 0), (1, 1), (3, 0), (3, 1), (2, 0), (2, 1)):
            r, c = along_y(dy, k)
            remote(slab_columns(r), mine, ss.at[0], rs.at[0], (r, c)).start()

    def slab_z():
        mine = slab.at[x, z_odd, z_hi]
        return [remote(mine, mine, ss.at[1], rs.at[1], along_z(dz, core)) for dz in (2, 1, 3)]

    def slab_x(p):
        piece = slab.at[x, lax.div(p, 4), lax.rem(lax.div(p, 2), 2), lax.rem(p, 2)]
        return [remote(piece, piece, ss.at[2], rs.at[2], along_x(dx)) for dx in (2, 1, 3)]

    def place(u):
        n = lax.rem(u, 8)
        mine = lax.div(9 - n, 8)
        e = (n - 2) * (1 - mine)
        c = 2 * lax.div(u, 8) + mine * n + (1 - mine) * lax.div(e, 3)
        return c, (1 - mine) * (lax.rem(e, 3) + 1)

    def own(c, l, to):
        first = pl.multiple_of((l * 4 + to) * block + c * width, width)
        return slopes.at[:, pl.ds(first, width)]

    def send_x(c, dx):
        for l in range(2):
            src = own(c, l, lax.rem(x + 4 - dx, 4))
            remote(src, held.at[c, dx - 1, l], sx.at[c], rx.at[c, dx - 1], along_x(4 - dx)).start()

    def send_y(u, block_of):
        dst = mid.at[u, y]
        for dy in ORDER:
            remote(block_of(lax.rem(y_lo + dy, 2)), dst, sy.at[u], ry.at[u], along_y(dy, core)).start()
        pltpu.make_async_copy(block_of(y_lo), dst, ry.at[u]).start()

    def z_copy(t, j, start):
        src = mid.at[t, pl.ds(2 * j, 2)]
        dst = tall.at[t, pl.ds(pl.multiple_of(z_odd * 4 + z_hi * 2, 2), 2)]
        to = 2 * j + core
        is_self = jnp.logical_and(to == z, core == z_odd)
        if start:

            @pl.when(is_self)
            def _():
                pltpu.make_async_copy(src, dst, rz.at[t]).start()

        @pl.when(jnp.logical_not(is_self))
        def _():
            copy = remote(src, dst, sz.at[t], rz.at[t], (y_hi * 2 + z_odd, to * 8 + y_lo * 4 + x))
            if start:
                copy.start()
            else:
                copy.wait_send()

    def group(t, g):
        return tall.at[t, pl.ds(pl.multiple_of(g * 4, 4), 4)]

    def forward(t):
        mine = group(t, core)
        return remote(mine, mine, sf.at[t], rf.at[t], along_y(0, other))

    def prepare():
        cov_copy.wait()
        wait_for(slab.at[pl.ds(0, 3)], rs.at[2])
        for part in range(4):
            whole = slab[part].reshape(deep, slab.shape[5]).T
            hi = whole.astype(jnp.bfloat16)
            slab_hi[part] = hi
            slab_lo[part] = (whole - hi.astype(jnp.float32)).astype(jnp.bfloat16)

    def compute(u):
        wait_for(group(u, other), rf.at[u])
        c, d = place(u)
        part = lax.rem(x + d, 4)
        unit = tall[u].reshape(deep, width)
        hi = unit.astype(jnp.bfloat16)
        lo = (unit - hi.astype(jnp.float32)).astype(jnp.bfloat16)
        dot = functools.partial(jnp.dot, preferred_element_type=jnp.float32)
        product = dot(slab_hi[part], hi) + dot(slab_hi[part], lo) + dot(slab_lo[part], hi)
        columns = pl.ds(pl.multiple_of(c * width, width), width)
        out[:, columns] = out[:, columns] + product * (1.0 / frames**0.5)

    send_y(0, lambda l: own(0, l, x))
    for dx in (1, 2, 3):
        send_x(0, dx)
    wait_for(slab.at[x, z_odd, z_hi], rs.at[0])
    for copy in slab_z():
        copy.start()
    for c in range(1, AHEAD):
        for dx in (1, 2, 3):
            send_x(c, dx)
    cov_copy.start()

    even = 2 * FIRST - LAG - 1

    @pl.loop(0, units + LAG)
    def _(s):
        c, d = place(s)

        @pl.when(jnp.logical_and(d == 0, jnp.logical_and(s > 0, s < units)))
        def _():
            send_y(s, lambda l: own(c, l, x))

        @pl.when(jnp.logical_and(d > 0, s < units))
        def _():
            wait_for(held.at[c, d - 1], rx.at[c, d - 1])
            send_y(s, lambda l: held.at[c, d - 1, l])

        @pl.when(jnp.logical_and(d > 0, c + AHEAD < units // 4))
        def _():
            send_x(c + AHEAD, d)

        @pl.when(s == SLAB_X)
        def _():
            wait_for(tall.at[0, pl.ds(0, 6)], rs.at[1])

        p = lax.div(s - SLAB_X, EVERY)

        @pl.when(jnp.logical_and(jnp.logical_and(s >= SLAB_X, p < 8), lax.rem(s - SLAB_X, EVERY) == 0))
        def _():
            for copy in slab_x(p):
                copy.start()

        @pl.when(jnp.logical_and(s >= LAG_Z, s < units + LAG_Z))
        def _():
            t = s - LAG_Z
            wait_for(mid.at[t], ry.at[t])
            for j in range(2):
                z_copy(t, j, True)

        @pl.when(s == FIRST)
        def _():
            prepare()

        @pl.when(jnp.logical_and(s >= FIRST, s < even))
        def _():
            for i in range(2):
                compute((s - FIRST) * 2 + i)

        @pl.when(s >= even)
        def _():
            compute(s - LAG - 1)

        @pl.when(s >= LAG)
        def _():
            t = s - LAG
            wait_for(group(t, core), rz.at[t])
            forward(t).start()

    compute(units - 1)

    @pl.when(is_source)
    def _():
        wait_for(tall.at[0, pl.ds(0, 7)], ss.at[0])

    for copy in slab_z():
        copy.wait_send()
    wait_for(slab.at[pl.ds(0, 3)], ss.at[2])

    @pl.loop(0, units // 4)
    def _(c):
        wait_for(held.at[c], sx.at[c])

    @pl.loop(0, units)
    def _(t):
        wait_for(mid.at[t, pl.ds(0, 3)], sy.at[t])
        for j in range(2):
            z_copy(t, j, False)
        forward(t).wait_send()


def per_device(slopes, covariance):
    frames, columns, rows = 1024, covariance.shape[1], covariance.shape[0]
    units = 4 * (columns // WIDTH)
    depth = slopes.shape[0]
    hbm = pl.BlockSpec(memory_space=pl.ANY)
    dma = pltpu.SemaphoreType.DMA
    return pl.pallas_call(
        kernel,
        out_shape=pltpu.VMEM(covariance.shape, jnp.float32),
        in_specs=[hbm, hbm],
        out_specs=pl.BlockSpec(memory_space=pltpu.VMEM),
        scratch_shapes=[
            pltpu.VMEM(slopes.shape, jnp.float32),
            pltpu.VMEM((units // 4, 3, 2, depth, WIDTH), jnp.float32),
            pltpu.VMEM((units, 4, depth, WIDTH), jnp.float32),
            pltpu.VMEM((units, 8, depth, WIDTH), jnp.float32),
            pltpu.VMEM((4, 2, 2, 2, depth, rows), jnp.float32),
            pltpu.VMEM((4, rows, frames // 4), jnp.bfloat16),
            pltpu.VMEM((4, rows, frames // 4), jnp.bfloat16),
            dma((units // 4,)), dma((units // 4, 3)),
        ] + [dma((units,))] * 6 + [dma((3,)), dma((3,)), dma, dma],
        compiler_params=pltpu.CompilerParams(
            collective_id=0, has_side_effects=True, vmem_limit_bytes=50 << 20
        ),
        cost_estimate=pl.CostEstimate(
            flops=6 * rows * frames * columns, bytes_accessed=24 << 20, transcendentals=0
        ),
        name="slab_update",
    )(slopes, covariance)


def solution(mesh):
    return jax.shard_map(
        per_device, mesh=mesh, in_specs=(P("col", "row"), P("row", "col")),
        out_specs=P("row", "col"), check_vma=False,
    )
```

time: 474 us -> 118 us (0.25); the launches traced: 468 us -> 117 us
  waiting for transfers between devices: 403 us -> 0 us
  Pallas kernels: 0 us -> 114 us
  matrix products: 32 us -> 0 us
  between operations: 13.4 us -> 0.01 us
  local copies, waits for them, and re-layouts: 13.1 us -> 3.4 us
  starting transfers between devices: 7.15 us -> 0 us
    all_gather x2 -> x0, waiting for transfers between devices: 402 us -> none  [the longest x1 286 us: per_device(): slab_all = lax.all_gather(slab_local, 'col', axis=0, tiled=True)]
    pallas_call x0 -> x1, Pallas kernels: none -> 114 us  [per_device(): pl.pallas_call(kernel, out_shape=pltpu.VMEM(covariance.shape, jnp.float32...]
    dot_general x1 -> x0, matrix products: 32 us -> none  [per_device(): lax.dot_general(slab_all, columns, (((0,), (0,)), ((), ())), precision=la...]
    all_to_all x1 -> x0, local copies, waits for them, and re-layouts: 11.6 us -> none  [per_device(): lax.all_to_all(gathered, 'col', split_axis=1, concat_axis=0, tiled=True)]
    all_to_all x1 -> x0, starting transfers between devices: 7.1 us -> none  [per_device(): lax.all_to_all(gathered, 'col', split_axis=1, concat_axis=0, tiled=True)]
  transfers between devices with their start and end apart: 3 -> 0, of which waited for: 2 -> 0; matrix products, arithmetic and copies ran while one was open for 0% -> 0% of each run, Pallas kernels for 0% -> 0%
where the time goes in v3:
time: 118 us; the launch traced here: 117 us
  Pallas kernels  114 us (97%)
  local copies, waits for them, and re-layouts  3.4 us (3%)
    pallas_call x1, Pallas kernels, per_device(): pl.pallas_call(kernel, out_shape=pltpu.VMEM(covariance.shape, jnp.float32...  114 us
    unnamed x1, local copies, waits for them, and re-layouts  3.4 us

profile of v3, /device:TPU:1, one launch (start us, length us, event | category | flops | bytes accessed | tf_op | source)
XLA Modules:
  0.0 117.3 jit_solution(7209329251646196980)
XLA Ops:
  0.0 113.9 %slab_update.1 = f32[512,4096]{1,0:T(8,128)S(1)} custom-call(f32[32,32768]{1,0:T(8,128)} %slopes_hbm.1, f32[512,4096]{1,0:T(8,128)} %cov.1), custom_call_target="tpu_custom_call" | custom-call | flops 12884901888 | bytes 25165824 | tf_op jit(solution)/shard_map/slab_update/pallas_call | solution.py:254
  113.9 3.4 %copy.4 = f32[512,4096]{1,0:T(8,128)} copy(f32[512,4096]{1,0:T(8,128)S(1)} %slab_update.1) | data formatting | bytes 16777216

commit v4 on v3

--- a/solution.py
+++ b/solution.py
@@ -167,6 +167,12 @@
             send_x(c, dx)
     cov_copy.start()
 
+    def sent(t):
+        wait_for(mid.at[t, pl.ds(0, 3)], sy.at[t])
+        for j in range(2):
+            z_copy(t, j, False)
+        forward(t).wait_send()
+
     even = 2 * FIRST - LAG - 1
 
     @pl.loop(0, units + LAG)
@@ -223,7 +229,9 @@
             wait_for(group(t, core), rz.at[t])
             forward(t).start()
 
-    compute(units - 1)
+        @pl.when(s > LAG)
+        def _():
+            sent(s - LAG - 1)
 
     @pl.when(is_source)
     def _():
@@ -237,12 +245,8 @@
     def _(c):
         wait_for(held.at[c], sx.at[c])
 
-    @pl.loop(0, units)
-    def _(t):
-        wait_for(mid.at[t, pl.ds(0, 3)], sy.at[t])
-        for j in range(2):
-            z_copy(t, j, False)
-        forward(t).wait_send()
+    compute(units - 1)
+    sent(units - 1)
 
 
 def per_device(slopes, covariance):

time: 118 us -> 117 us (level)
  no operation moved by 1% of the time
where the time goes in v4:
time: 117 us
  Pallas kernels  113 us (97%)
  local copies, waits for them, and re-layouts  3.4 us (3%)
    pallas_call x1, Pallas kernels, per_device(): pl.pallas_call(kernel, out_shape=pltpu.VMEM(covariance.shape, jnp.float32...  113 us
    unnamed x1, local copies, waits for them, and re-layouts  3.4 us

profile of v4, /device:TPU:1, one launch (start us, length us, event | category | flops | bytes accessed | tf_op | source)
XLA Modules:
  0.0 116.8 jit_solution(4603178378403226945)
XLA Ops:
  0.0 113.4 %slab_update.1 = f32[512,4096]{1,0:T(8,128)S(1)} custom-call(f32[32,32768]{1,0:T(8,128)} %slopes_hbm.1, f32[512,4096]{1,0:T(8,128)} %cov.1), custom_call_target="tpu_custom_call" | custom-call | flops 12884901888 | bytes 25165824 | tf_op jit(solution)/shard_map/slab_update/pallas_call | solution.py:258
  113.4 3.4 %copy.4 = f32[512,4096]{1,0:T(8,128)} copy(f32[512,4096]{1,0:T(8,128)S(1)} %slab_update.1) | data formatting | bytes 16777216
